TPU v7x, 32 devices: a whole 2x2x4 slice. The times are simulated.
32 devices in a mesh: dp: 4 (over y, core), expert: 8 (over z, x).
Axes of the slice: x: 2, y: 2, z: 4, core: 2. Of those that a mesh axis runs over, the one named last changes fastest.
Arguments:
- tokens: bfloat16 [4096, 1024], P(('dp', 'expert')), may hold values from -6 to 6
- routes: int32 [4096, 4], P(('dp', 'expert')), may hold values from 0 to 7, all different within a row; in each aligned block of 128 rows (0 to 127, 128 to 255, ...) at most 128 rows name the same one
- gates: float32 [4096, 4], P(('dp', 'expert')), may hold values from 0.05 to 0.5
- w_in: bfloat16 [8, 1024, 768], P('expert', 'dp'), may hold values from -6 to 6
- w_down: bfloat16 [8, 384, 1024], P('expert', 'dp'), may hold values from -6 to 6
- out_grad: bfloat16 [4096, 1024], P(('dp', 'expert')), may hold values from -6 to 6
Outputs:
- moe_out: bfloat16 [4096, 1024], P(('dp', 'expert'))
- token_grad: bfloat16 [4096, 1024], P(('dp', 'expert'))
- new_w_in: bfloat16 [8, 1024, 768], P('expert', 'dp')
- new_w_down: bfloat16 [8, 384, 1024], P('expert', 'dp')
Inputs may be any that keep to these rules, and one draw needn't show every extreme that they name: `routes`: within one device's 128 tokens no expert is named more than 128 times, a bound that some block reaches; a token names 4 different experts.
All inputs are finite; a program needn't handle non-finite values.
Results may differ from a plain program's by a relative error of at most 0.014.
Values may be sent and summed in bfloat16 or wider, within the bound.
A program may use at most 64 MiB of HBM per device.

v0:
```python
import jax
import jax.numpy as jnp
from jax import lax
from jax.sharding import PartitionSpec as P

step_rate = 0.5


def slot_numbers(route_rows, experts, capacity):
    flat_routes = route_rows.reshape(-1)
    one_hot = (flat_routes[:, None] == jnp.arange(experts, dtype=jnp.int32)[None, :]).astype(
        jnp.int32
    )
    running = jnp.cumsum(one_hot, axis=0)
    position = jnp.sum(one_hot * running, axis=1) - 1
    return flat_routes * capacity + position


def expert_forward(inputs, full_in, full_down):
    model_width = full_in.shape[1]
    hidden_units = full_down.shape[1]
    projected = jnp.einsum(
        "sxcd,xdj->sxcj", inputs, full_in, preferred_element_type=jnp.float32
    ) * model_width ** (-0.5)
    gate_part = projected[..., :hidden_units]
    up_part = projected[..., hidden_units:]
    activation = (jax.nn.silu(gate_part) * up_part).astype(jnp.bfloat16)
    results = (
        jnp.einsum("sxcf,xfd->sxcd", activation, full_down, preferred_element_type=jnp.float32)
        * hidden_units ** (-0.5)
    ).astype(jnp.bfloat16)
    return (projected, activation, results)


def expert_backward(projected, grad_rows, full_in, full_down):
    model_width = full_in.shape[1]
    hidden_units = full_down.shape[1]
    grad_act = jnp.einsum(
        "sxcd,xfd->sxcf", grad_rows, full_down, preferred_element_type=jnp.float32
    ) * hidden_units ** (-0.5)
    gate_part = projected[..., :hidden_units]
    up_part = projected[..., hidden_units:]
    sigmoid_gate = jax.nn.sigmoid(gate_part)
    grad_gate = grad_act * up_part * sigmoid_gate * (1.0 + gate_part * (1.0 - sigmoid_gate))
    grad_up = grad_act * jax.nn.silu(gate_part)
    grad_hidden = jnp.concatenate([grad_gate, grad_up], axis=-1).astype(jnp.bfloat16)
    grad_inputs = (
        jnp.einsum("sxcj,xdj->sxcd", grad_hidden, full_in, preferred_element_type=jnp.float32)
        * model_width ** (-0.5)
    ).astype(jnp.bfloat16)
    return (grad_hidden, grad_inputs)


def body(tokens, routes, gates, w_in, w_down, out_grad):
    tok_rows, model_width = tokens.shape
    top_count = routes.shape[1]
    per_device = w_in.shape[0]
    hidden_units = w_down.shape[2] and w_in.shape[2] // 2
    sources = lax.axis_size("expert")
    experts = per_device * sources
    capacity = min(tok_rows, 2 * tok_rows * top_count // experts)
    slot_index = slot_numbers(routes, experts, capacity)
    token_of = jnp.arange(tok_rows * top_count, dtype=jnp.int32) // top_count
    layout = (sources, per_device, capacity, model_width)
    send_inputs = (
        jnp.zeros((experts * capacity, model_width), jnp.bfloat16)
        .at[slot_index]
        .set(tokens[token_of])
        .reshape(layout)
    )
    scaled = (gates.reshape(-1)[:, None] * out_grad[token_of].astype(jnp.float32)).astype(
        jnp.bfloat16
    )
    send_grads = (
        jnp.zeros((experts * capacity, model_width), jnp.bfloat16)
        .at[slot_index]
        .set(scaled)
        .reshape(layout)
    )
    full_in, full_down = (
        lax.all_gather(w_in, "dp", axis=1, tiled=True),
        lax.all_gather(w_down, "dp", axis=1, tiled=True),
    )
    inputs_here = lax.all_to_all(send_inputs, "expert", split_axis=0, concat_axis=0, tiled=True)
    projected_here, activation_here, results_here = expert_forward(inputs_here, full_in, full_down)
    results_home = lax.all_to_all(results_here, "expert", split_axis=0, concat_axis=0, tiled=True)
    grad_rows = lax.all_to_all(send_grads, "expert", split_axis=0, concat_axis=0, tiled=True)
    grad_hidden, grad_inputs = expert_backward(projected_here, grad_rows, full_in, full_down)
    inputs_back = lax.all_to_all(grad_inputs, "expert", split_axis=0, concat_axis=0, tiled=True)
    picked = results_home.reshape(experts * capacity, model_width)[slot_index].astype(jnp.float32)
    picked = picked.reshape(tok_rows, top_count, model_width)
    moe_out = jnp.sum(picked * gates[:, :, None], axis=1).astype(jnp.bfloat16)
    back_rows = inputs_back.reshape(experts * capacity, model_width)[slot_index].astype(jnp.float32)
    token_grad = jnp.sum(back_rows.reshape(tok_rows, top_count, model_width), axis=1).astype(
        jnp.bfloat16
    )
    column_part = inputs_here
    summed_in = lax.psum_scatter(
        (
            jnp.einsum(
                "sxcd,sxcj->dxj", column_part, grad_hidden, preferred_element_type=jnp.float32
            )
            * model_width ** (-0.5)
        ).astype(jnp.bfloat16),
        "dp",
        scatter_dimension=0,
        tiled=True,
    ).astype(jnp.float32)
    column_part = activation_here
    summed_down = lax.psum_scatter(
        (
            jnp.einsum("sxcf,sxcd->fxd", column_part, grad_rows, preferred_element_type=jnp.float32)
            * hidden_units ** (-0.5)
        ).astype(jnp.bfloat16),
        "dp",
        scatter_dimension=0,
        tiled=True,
    ).astype(jnp.float32)
    new_w_in = (w_in.astype(jnp.float32) - step_rate * jnp.transpose(summed_in, (1, 0, 2))).astype(
        jnp.bfloat16
    )
    new_w_down = (
        w_down.astype(jnp.float32) - step_rate * jnp.transpose(summed_down, (1, 0, 2))
    ).astype(jnp.bfloat16)
    return (moe_out, token_grad, new_w_in, new_w_down)


def solution(mesh):
    return jax.shard_map(
        body,
        mesh=mesh,
        in_specs=(
            P(("dp", "expert"), None),
            P(("dp", "expert"), None),
            P(("dp", "expert"), None),
            P("expert", "dp", None),
            P("expert", "dp", None),
            P(("dp", "expert"), None),
        ),
        out_specs=(
            P(("dp", "expert"), None),
            P(("dp", "expert"), None),
            P("expert", "dp", None),
            P("expert", "dp", None),
        ),
        check_vma=False,
    )
```

profile of v0, /device:TPU:8, one launch (start us, length us, event | category | flops | bytes accessed | tf_op | source)
XLA Modules:
  0.0 250.5 jit_solution(13568643230272533931)
XLA Ops:
  10.7 7.7 %scatter_custom_fusion = bf16[1024,1024]{1,0:T(8,128)(2,1)} fusion(s32[512]{0:T(512)S(1)} %bitcast.134, bf16[128,1024]{1,0:T(8,128)(2,1)S(1)} %copy-done, s32[1024]{0:T(1024)S(1)} %pad_clamp_fusion.1, bf16[]{:T(256)} %constant.17.clone.1), kind=kCustom, calls=%fused_computation.41 | custom fusion | bytes 2097154 | tf_op jit(solution)/shard_map/scatter | solution.py:68
  18.5 6.4 %all-to-all-start = ((bf16[8,1,128,1024]{3,2,1,0:T(8,128)(2,1)}), bf16[8,1,128,1024]{3,2,1,0:T(8,128)(2,1)S(1)}, u32[]{:S(2)}, u32[]{:S(2)}) async-start(bf16[8,1,128,1024]{3,2,1,0:T(8,128)(2,1)} %bitcast.5), calls=%async_computation | async-start | bytes 4194304 | tf_op jit(solution)/shard_map/all_to_all | solution.py:84
  25.1 7.8 %scatter_custom_fusion.1 = bf16[1024,1024]{1,0:T(8,128)(2,1)} fusion(s32[512]{0:T(512)S(1)} %bitcast.135, f32[512]{0:T(512)S(1)} %mul.169, bf16[]{:T(256)} %constant.17.clone.1, bf16[128,1024]{1,0:T(8,128)(2,1)S(1)} %copy-done.5, s32[1024]{0:T(1024)S(1)} %pad_clamp_fusion.1), kind=kCustom, calls=%fused_computation.40 | custom fusion | flops 1572864 | bytes 2365442 | tf_op jit(solution)/shard_map/scatter | solution.py:77
  32.9 37.7 %all-to-all-done = bf16[8,1,128,1024]{3,2,1,0:T(8,128)(2,1)S(1)} async-done(((bf16[8,1,128,1024]{3,2,1,0:T(8,128)(2,1)}), bf16[8,1,128,1024]{3,2,1,0:T(8,128)(2,1)S(1)}, u32[]{:S(2)}, u32[]{:S(2)}) %all-to-all-start) | async-done | bytes 2097184 | tf_op jit(solution)/shard_map/all_to_all | solution.py:84
  70.6 6.8 %all-to-all-start.2 = ((bf16[8,1,128,1024]{3,2,1,0:T(8,128)(2,1)}), bf16[8,1,128,1024]{3,2,1,0:T(8,128)(2,1)}, u32[]{:S(2)}, u32[]{:S(2)}) async-start(bf16[8,1,128,1024]{3,2,1,0:T(8,128)(2,1)} %bitcast.22), calls=%async_computation.2 | async-start | bytes 4194304 | tf_op jit(solution)/shard_map/all_to_all | solution.py:87
  78.2 8.6 %all_gather.7 = bf16[1,384,1024]{2,1,0:T(8,128)(2,1)S(1)} all-gather(bf16[1,96,1024]{2,1,0:T(8,128)(2,1)S(1)} %copy-done.4), channel_id=1, replica_groups=mesh['dp'=4,'expert'=8] {'dp'}, dimensions={1}, use_global_device_ids=true | all-gather | bytes 983040 | tf_op jit(solution)/shard_map/all_gather | solution.py:82
  86.8 13.7 %all-gather.2.cloned.1.call-done = bf16[1,1024,768]{2,1,0:T(8,128)(2,1)} async-done(((bf16[1,256,768]{2,1,0:T(8,128)(2,1)}), bf16[1,1024,768]{2,1,0:T(8,128)(2,1)}) %all-gather.2.cloned.1.call-update) | async-done | bytes 1572880 | tf_op jit(solution)/shard_map/all_gather | solution.py:81
  100.5 4.9 %multiply_bitcast_fusion = f32[8,1,128,768]{3,2,0,1:T(8,128)} fusion(bf16[8,1,128,1024]{3,2,1,0:T(8,128)(2,1)S(1)} %all-to-all-done, bf16[1,1024,768]{2,1,0:T(8,128)(2,1)} %all-gather.2.cloned.1.call-done), kind=kOutput, calls=%fused_computation.10 | convolution fusion | flops 1611399168 | bytes 6815744 | tf_op jit(solution)/shard_map/sxcd,xdj->sxcj/dot_general | solution.py:22
  105.4 17.3 %all-to-all-done.2 = bf16[8,1,128,1024]{3,2,1,0:T(8,128)(2,1)} async-done(((bf16[8,1,128,1024]{3,2,1,0:T(8,128)(2,1)}), bf16[8,1,128,1024]{3,2,1,0:T(8,128)(2,1)}, u32[]{:S(2)}, u32[]{:S(2)}) %all-to-all-start.2) | async-done | bytes 2097184 | tf_op jit(solution)/shard_map/all_to_all | solution.py:87
  122.7 5.2 %fusion.45 = (bf16[8,128,384]{2,1,0:T(8,128)(2,1)S(1)}, bf16[8,128,384]{2,1,0:T(8,128)(2,1)S(1)}, bf16[8,128,384]{2,1,0:T(8,128)(2,1)}) fusion(f32[8,1,128,768]{3,2,0,1:T(8,128)} %multiply_bitcast_fusion, bf16[1,384,1024]{2,1,0:T(8,128)(2,1)S(1)} %all_gather.7, bf16[8,1,128,1024]{3,2,1,0:T(8,128)(2,1)} %all-to-all-done.2), kind=kOutput, calls=%fused_computation.52 | convolution fusion | flops 811597824 | bytes 8388608 | tf_op jit(solution)/shard_map/sxcd,xfd->sxcf/dot_general | solution.py:38
  129.1 3.2 %fusion.14 = bf16[8,1,128,1024]{3,2,1,0:T(8,128)(2,1)} fusion(bf16[1,1024,768]{2,1,0:T(8,128)(2,1)S(1)} %copy-done.7, bf16[8,128,384]{2,1,0:T(8,128)(2,1)S(1)} %get-tuple-element.17, bf16[8,128,384]{2,1,0:T(8,128)(2,1)S(1)} %get-tuple-element.16), kind=kOutput, calls=%fused_computation.22 | convolution fusion | flops 1615855616 | bytes 5242880 | tf_op jit(solution)/shard_map/sxcj,xdj->sxcd/dot_general | solution.py:48
  132.3 6.3 %all-to-all-start.3 = ((bf16[8,1,128,1024]{3,2,1,0:T(8,128)(2,1)}), bf16[8,1,128,1024]{3,2,1,0:T(8,128)(2,1)S(1)}, u32[]{:S(2)}, u32[]{:S(2)}) async-start(bf16[8,1,128,1024]{3,2,1,0:T(8,128)(2,1)} %fusion.14), calls=%async_computation.3 | async-start | bytes 4194304 | tf_op jit(solution)/shard_map/all_to_all | solution.py:89
  138.7 3.0 %fusion.31 = bf16[384,1024]{0,1:T(8,128)(2,1)S(1)} fusion(bf16[8,128,384]{2,1,0:T(8,128)(2,1)} %get-tuple-element.18, bf16[8,1,128,1024]{3,2,1,0:T(8,128)(2,1)} %all-to-all-done.2), kind=kOutput, calls=%fused_computation.39 | convolution fusion | flops 806092800 | bytes 3670016 | tf_op jit(solution)/shard_map/sxcf,sxcd->fxd/dot_general | solution.py:112
  142.9 4.0 %fusion.13 = bf16[8,1,128,1024]{3,2,1,0:T(8,128)(2,1)} fusion(bf16[8,128,384]{2,1,0:T(8,128)(2,1)} %get-tuple-element.18, bf16[1,384,1024]{2,1,0:T(8,128)(2,1)} %copy-done.3), kind=kOutput, calls=%fused_computation.21 | convolution fusion | flops 807403520 | bytes 3670016 | tf_op jit(solution)/shard_map/sxcf,xfd->sxcd/dot_general | solution.py:29
  146.9 37.7 %all-to-all-done.3 = bf16[8,1,128,1024]{3,2,1,0:T(8,128)(2,1)S(1)} async-done(((bf16[8,1,128,1024]{3,2,1,0:T(8,128)(2,1)}), bf16[8,1,128,1024]{3,2,1,0:T(8,128)(2,1)S(1)}, u32[]{:S(2)}, u32[]{:S(2)}) %all-to-all-start.3) | async-done | bytes 2097184 | tf_op jit(solution)/shard_map/all_to_all | solution.py:89
  184.6 6.7 %all-to-all-start.1 = ((bf16[8,1,128,1024]{3,2,1,0:T(8,128)(2,1)}), bf16[8,1,128,1024]{3,2,1,0:T(8,128)(2,1)}, u32[]{:S(2)}, u32[]{:S(2)}) async-start(bf16[8,1,128,1024]{3,2,1,0:T(8,128)(2,1)} %fusion.13), calls=%async_computation.1 | async-start | bytes 4194304 | tf_op jit(solution)/shard_map/all_to_all | solution.py:86
  191.4 5.2 %fusion.28 = bf16[1024,1,768]{0,2,1:T(8,128)(2,1)} fusion(bf16[8,1,128,1024]{3,2,1,0:T(8,128)(2,1)} %copy-done.1, bf16[8,128,384]{2,1,0:T(8,128)(2,1)} %copy-done.9, bf16[8,128,384]{2,1,0:T(8,128)(2,1)} %copy-done.8), kind=kOutput, calls=%fused_computation.38 | convolution fusion | flops 1615331328 | bytes 5242880 | tf_op jit(solution)/shard_map/sxcd,sxcj->dxj/dot_general | solution.py:100
  198.9 1.8 copy.40
  200.6 25.2 %reduce-scatter.5.cloned.1.call-done = bf16[256,1,768]{0,2,1:T(8,128)(2,1)} async-done(((bf16[1024,1,768]{0,2,1:T(8,128)(2,1)}), bf16[256,1,768]{0,2,1:T(8,128)(2,1)}) %reduce-scatter.5.cloned.1.call-update) | async-done | bytes 393232 | tf_op jit(solution)/shard_map/reduce_scatter | solution.py:98
  227.8 2.0 gather_fusion.1
  230.3 2.1 reduce_sum.32
  232.4 4.1 %all-to-all-done.1 = bf16[8,1,128,1024]{3,2,1,0:T(8,128)(2,1)} async-done(((bf16[8,1,128,1024]{3,2,1,0:T(8,128)(2,1)}), bf16[8,1,128,1024]{3,2,1,0:T(8,128)(2,1)}, u32[]{:S(2)}, u32[]{:S(2)}) %all-to-all-start.1) | async-done | bytes 2097184 | tf_op jit(solution)/shard_map/all_to_all | solution.py:86
  236.5 4.6 %gather_fusion = bf16[512,1024]{1,0:T(8,128)(2,1)S(1)} fusion(bf16[1024,1024]{1,0:T(8,128)(2,1)} %bitcast.21, s32[1024]{0:T(1024)S(1)} %pad_clamp_fusion), kind=kCustom, calls=%fused_computation.1 | custom fusion | bytes 2099200 | tf_op jit(solution)/shard_map/gather | solution.py:90
  241.9 2.1 multiply_reduce_fusion
  (55 shorter events, 12.3 us)
Async XLA Ops:
  7.2 3.5 %copy-start = (bf16[128,1024]{1,0:T(8,128)(2,1)S(1)}, bf16[128,1024]{1,0:T(8,128)(2,1)}, u32[]{:S(2)}) copy-start(bf16[128,1024]{1,0:T(8,128)(2,1)} %param.6) | copy-start | bytes 786436
  18.5 6.4 %copy-start.6 = (f32[128,4]{0,1:T(4,128)S(1)}, f32[128,4]{0,1:T(4,128)}, u32[]{:S(2)}) copy-start(f32[128,4]{0,1:T(4,128)} %param.8) | copy-start | bytes 6148
  18.5 6.6 %copy-start.5 = (bf16[128,1024]{1,0:T(8,128)(2,1)S(1)}, bf16[128,1024]{1,0:T(8,128)(2,1)}, u32[]{:S(2)}) copy-start(bf16[128,1024]{1,0:T(8,128)(2,1)} %param.11) | copy-start | bytes 786436
  18.5 52.2 %all-to-all-start = ((bf16[8,1,128,1024]{3,2,1,0:T(8,128)(2,1)}), bf16[8,1,128,1024]{3,2,1,0:T(8,128)(2,1)S(1)}, u32[]{:S(2)}, u32[]{:S(2)}) async-start(bf16[8,1,128,1024]{3,2,1,0:T(8,128)(2,1)} %bitcast.5), calls=%async_computation | async-start | bytes 4194304 | tf_op jit(solution)/shard_map/all_to_all | solution.py:84
  70.6 29.9 %copy-start.1 = (bf16[8,1,128,1024]{3,2,1,0:T(8,128)(2,1)}, bf16[8,1,128,1024]{3,2,1,0:T(8,128)(2,1)S(1)}, u32[]{:S(2)}) copy-start(bf16[8,1,128,1024]{3,2,1,0:T(8,128)(2,1)S(1)} %all-to-all-done) | copy-start | bytes 6291460
  70.6 7.6 %copy-start.4 = (bf16[1,96,1024]{2,1,0:T(8,128)(2,1)S(1)}, bf16[1,96,1024]{2,1,0:T(8,128)(2,1)}, u32[]{:S(2)}) copy-start(bf16[1,96,1024]{2,1,0:T(8,128)(2,1)} %param.10) | copy-start | bytes 589828
  70.6 52.0 %all-to-all-start.2 = ((bf16[8,1,128,1024]{3,2,1,0:T(8,128)(2,1)}), bf16[8,1,128,1024]{3,2,1,0:T(8,128)(2,1)}, u32[]{:S(2)}, u32[]{:S(2)}) async-start(bf16[8,1,128,1024]{3,2,1,0:T(8,128)(2,1)} %bitcast.22), calls=%async_computation.2 | async-start | bytes 4194304 | tf_op jit(solution)/shard_map/all_to_all | solution.py:87
  77.5 23.0 %all-gather.2.cloned.1.call-start = ((), (), s32[]{:S(2)}) async-start(), calls=%async_computation.6 | async-start | bytes 1966080 | tf_op jit(solution)/shard_map/all_gather | solution.py:81
  86.8 35.8 %copy-start.3 = (bf16[1,384,1024]{2,1,0:T(8,128)(2,1)}, bf16[1,384,1024]{2,1,0:T(8,128)(2,1)S(1)}, u32[]{:S(2)}) copy-start(bf16[1,384,1024]{2,1,0:T(8,128)(2,1)S(1)} %all_gather.7) | copy-start | bytes 2359300
  105.3 23.8 %copy-start.7 = (bf16[1,1024,768]{2,1,0:T(8,128)(2,1)S(1)}, bf16[1,1024,768]{2,1,0:T(8,128)(2,1)}, u32[]{:S(2)}) copy-start(bf16[1,1024,768]{2,1,0:T(8,128)(2,1)} %all-gather.2.cloned.1.call-done) | copy-start | bytes 4718596
  127.9 0.9 copy-start.8
  127.9 1.2 copy-start.9
  132.3 52.3 %all-to-all-start.3 = ((bf16[8,1,128,1024]{3,2,1,0:T(8,128)(2,1)}), bf16[8,1,128,1024]{3,2,1,0:T(8,128)(2,1)S(1)}, u32[]{:S(2)}, u32[]{:S(2)}) async-start(bf16[8,1,128,1024]{3,2,1,0:T(8,128)(2,1)} %fusion.14), calls=%async_computation.3 | async-start | bytes 4194304 | tf_op jit(solution)/shard_map/all_to_all | solution.py:89
  138.7 58.3 %reduce-scatter.7.cloned.1.call-start = ((), (), s32[]{:S(2)}) async-start(), calls=%async_computation.8 | async-start | bytes 983040
  184.6 51.9 %all-to-all-start.1 = ((bf16[8,1,128,1024]{3,2,1,0:T(8,128)(2,1)}), bf16[8,1,128,1024]{3,2,1,0:T(8,128)(2,1)}, u32[]{:S(2)}, u32[]{:S(2)}) async-start(bf16[8,1,128,1024]{3,2,1,0:T(8,128)(2,1)} %fusion.13), calls=%async_computation.1 | async-start | bytes 4194304 | tf_op jit(solution)/shard_map/all_to_all | solution.py:86
  191.4 5.2 %copy-start.2 = (bf16[1,256,768]{2,1,0:T(8,128)(2,1)S(1)}, bf16[1,256,768]{2,1,0:T(8,128)(2,1)}, u32[]{:S(2)}) copy-start(bf16[1,256,768]{2,1,0:T(8,128)(2,1)} %param.9) | copy-start | bytes 1179652
  191.4 34.5 %reduce-scatter.5.cloned.1.call-start = ((), (), s32[]{:S(2)}) async-start(), calls=%async_computation.7 | async-start | bytes 1966080 | tf_op jit(solution)/shard_map/reduce_scatter | solution.py:98
Sparse Core Ops, SparseCore 0:
  79.9 20.5 all-gather.1
  143.1 24.1 reduce-scatter.6
  196.7 29.0 reduce-scatter.4
where the time goes:
time: 255 us; the launch traced here: 250 us
  waiting for transfers between devices  136 us (53%)
  starting transfers between devices  26.3 us (10%)
  matrix products  25.5 us (10%)
  local copies, waits for them, and re-layouts  23.7 us (9%)
  other arithmetic  15.9 us (6%)
  between operations  13.9 us (5%)
  blocking collectives  8.63 us (3%)
    all_to_all x1, waiting for transfers between devices, body(): lax.all_to_all(grad_inputs, 'expert', split_axis=0, concat_axis=0, tiled=...  37.7 us
    all_to_all x1, waiting for transfers between devices, body(): lax.all_to_all(send_inputs, 'expert', split_axis=0, concat_axis=0, tiled=...  37.7 us
    reduce_scatter x1, waiting for transfers between devices, body(): lax.psum_scatter((jnp.einsum('sxcd,sxcj->dxj', column_part, grad_hidden,...  25.2 us
    all_to_all x1, waiting for transfers between devices, body(): lax.all_to_all(send_grads, 'expert', split_axis=0, concat_axis=0, tiled=T...  17.3 us
    all_gather x1, waiting for transfers between devices, body(): lax.all_gather(w_in, 'dp', axis=1, tiled=True)  13.7 us
    all_gather x1, blocking collectives, body(): lax.all_gather(w_down, 'dp', axis=1, tiled=True)  8.63 us
    scatter x1, other arithmetic, body(): send_grads = jnp.zeros((experts * capacity, model_width), jnp.bfloat16).a...  7.85 us
    scatter x1, local copies, waits for them, and re-layouts, body(): send_inputs = jnp.zeros((experts * capacity, model_width), jnp.bfloat16)....  7.75 us
  transfers between devices with their start and end apart: 7, of which 6 were waited for; matrix products, arithmetic and copies ran while one was open for 15% of the time, Pallas kernels for 0%

commit v1 on v0

v1 whole, which is shorter than its diff:
```python
import jax
import jax.numpy as jnp
from jax import lax
from jax.sharding import PartitionSpec as P

step_rate = 0.5


def expert_gates(routes, gates, experts):
    hit = routes[:, :, None] == jnp.arange(experts, dtype=jnp.int32)[None, None, :]
    return jnp.sum(jnp.where(hit, gates[:, :, None], 0.0), axis=1)


def body(tokens, routes, gates, w_in, w_down, out_grad):
    model_width = tokens.shape[1]
    hidden = w_in.shape[2] // 2
    per_device = w_in.shape[0]
    experts = per_device * lax.axis_size("expert")
    scale_in = model_width**-0.5
    scale_down = hidden**-0.5
    f32 = jnp.float32
    full_in = lax.all_gather(w_in, "dp", axis=1, tiled=True)
    all_tokens = lax.all_gather(tokens, "expert", axis=0, tiled=True)
    all_grads = lax.all_gather(out_grad, "expert", axis=0, tiled=True)
    full_down = lax.all_gather(w_down, "dp", axis=1, tiled=True)
    weight = lax.all_gather(expert_gates(routes, gates, experts), "expert", axis=0, tiled=True)
    first = lax.axis_index("expert") * per_device
    moe, back, grads_in, grads_down = 0.0, 0.0, [], []
    for local in range(per_device):
        win, wdown = full_in[local], full_down[local]
        g = lax.dynamic_slice_in_dim(weight, first + local, 1, axis=1)
        proj = jnp.dot(all_tokens, win, preferred_element_type=f32) * scale_in
        gate, up = proj[:, :hidden], proj[:, hidden:]
        sig = jax.nn.sigmoid(gate)
        act = (gate * sig * up).astype(jnp.bfloat16)
        y = (jnp.dot(act, wdown, preferred_element_type=f32) * scale_down).astype(jnp.bfloat16)
        moe = moe + g * y.astype(f32)
        dy = (g * all_grads.astype(f32)).astype(jnp.bfloat16)
        dact = lax.dot_general(dy, wdown, (((1,), (1,)), ((), ())), preferred_element_type=f32) * scale_down
        dproj = jnp.concatenate(
            [dact * up * sig * (1.0 + gate * (1.0 - sig)), dact * gate * sig], axis=-1
        ).astype(jnp.bfloat16)
        dx = lax.dot_general(dproj, win, (((1,), (1,)), ((), ())), preferred_element_type=f32) * scale_in
        back = back + dx.astype(jnp.bfloat16).astype(f32)
        grads_in.append(
            (lax.dot_general(all_tokens, dproj, (((0,), (0,)), ((), ())), preferred_element_type=f32) * scale_in).astype(jnp.bfloat16)
        )
        grads_down.append(
            (lax.dot_general(act, dy, (((0,), (0,)), ((), ())), preferred_element_type=f32) * scale_down).astype(jnp.bfloat16)
        )
    moe_out = lax.psum_scatter(moe.astype(jnp.bfloat16), "expert", scatter_dimension=0, tiled=True)
    token_grad = lax.psum_scatter(back.astype(jnp.bfloat16), "expert", scatter_dimension=0, tiled=True)
    sum_in = lax.psum_scatter(jnp.stack(grads_in), "dp", scatter_dimension=1, tiled=True)
    sum_down = lax.psum_scatter(jnp.stack(grads_down), "dp", scatter_dimension=1, tiled=True)
    new_w_in = (w_in.astype(f32) - step_rate * sum_in.astype(f32)).astype(jnp.bfloat16)
    new_w_down = (w_down.astype(f32) - step_rate * sum_down.astype(f32)).astype(jnp.bfloat16)
    return (moe_out, token_grad, new_w_in, new_w_down)


def solution(mesh):
    return jax.shard_map(
        body,
        mesh=mesh,
        in_specs=(
            P(("dp", "expert"), None),
            P(("dp", "expert"), None),
            P(("dp", "expert"), None),
            P("expert", "dp", None),
            P("expert", "dp", None),
            P(("dp", "expert"), None),
        ),
        out_specs=(
            P(("dp", "expert"), None),
            P(("dp", "expert"), None),
            P("expert", "dp", None),
            P("expert", "dp", None),
        ),
        check_vma=False,
    )
```

time: 255 us -> 345 us (1.35)
  waiting for transfers between devices: 136 us -> 258 us
  blocking collectives: 8.63 us -> 36.8 us
  starting transfers between devices: 26.3 us -> 0.28 us
  local copies, waits for them, and re-layouts: 23.7 us -> 4.03 us
  other arithmetic: 15.9 us -> 3.49 us
    reduce_scatter x1 -> x4, waiting for transfers between devices: 25.2 us -> 177 us  [the longest x1 70.9 us: body(): lax.psum_scatter(moe.astype(jnp.bfloat16), 'expert', scatter_dimension=0,...]
    all_to_all x4 -> x0, waiting for transfers between devices: 96.9 us -> none  [the longest x1 37.7 us: body(): lax.all_to_all(grad_inputs, 'expert', split_axis=0, concat_axis=0, tiled=...]
    all_gather x1 -> x3, waiting for transfers between devices: 13.7 us -> 79.4 us  [the longest x1 44.4 us: body(): all_grads = lax.all_gather(out_grad, 'expert', axis=0, tiled=True)]
    all_gather x1 -> x2, blocking collectives: 8.63 us -> 36.8 us  [the longest x1 27.9 us: body(): lax.all_gather(expert_gates(routes, gates, experts), 'expert', axis=0, ti...]
    all_to_all x4 -> x0, starting transfers between devices: 26.3 us -> none  [the longest x1 6.84 us: body(): lax.all_to_all(send_grads, 'expert', split_axis=0, concat_axis=0, tiled=T...]
    scatter x1 -> x0, other arithmetic: 7.85 us -> none  [body(): send_grads = jnp.zeros((experts * capacity, model_width), jnp.bfloat16).a...]
    scatter x1 -> x0, local copies, waits for them, and re-layouts: 7.75 us -> none  [body(): send_inputs = jnp.zeros((experts * capacity, model_width), jnp.bfloat16)....]
    gather x3 -> x0, local copies, waits for them, and re-layouts: 7.07 us -> none  [the longest x1 4.59 us: body(): results_home.reshape(experts * capacity, model_width)[slot_index]]
  transfers between devices with their start and end apart: 7 -> 7, of which waited for: 6 -> 6; matrix products, arithmetic and copies ran while one was open for 15% -> 7% of each run, Pallas kernels for 0% -> 0%
where the time goes in v1:
time: 345 us; the launch traced here: 342 us
  waiting for transfers between devices  258 us (75%)
  blocking collectives  36.8 us (11%)
  matrix products  25.3 us (7%)
  between operations  14.2 us (4%)
  local copies, waits for them, and re-layouts  4.03 us (1%)
  other arithmetic  3.49 us (1%)
    reduce_scatter x1, waiting for transfers between devices, body(): lax.psum_scatter(moe.astype(jnp.bfloat16), 'expert', scatter_dimension=0,...  70.9 us
    reduce_scatter x1, waiting for transfers between devices, body(): lax.psum_scatter(back.astype(jnp.bfloat16), 'expert', scatter_dimension=0...  69.2 us
    all_gather x1, waiting for transfers between devices, body(): all_grads = lax.all_gather(out_grad, 'expert', axis=0, tiled=True)  44.4 us
    all_gather x1, waiting for transfers between devices, body(): all_tokens = lax.all_gather(tokens, 'expert', axis=0, tiled=True)  34.9 us
    reduce_scatter x1, waiting for transfers between devices, body(): lax.psum_scatter(jnp.stack(grads_in), 'dp', scatter_dimension=1, tiled=True)  29.1 us
    all_gather x1, blocking collectives, body(): lax.all_gather(expert_gates(routes, gates, experts), 'expert', axis=0, ti...  27.9 us
    all_gather x1, blocking collectives, body(): full_down = lax.all_gather(w_down, 'dp', axis=1, tiled=True)  8.84 us
    reduce_scatter x1, waiting for transfers between devices, body(): lax.psum_scatter(jnp.stack(grads_down), 'dp', scatter_dimension=1, tiled=...  7.3 us
  transfers between devices with their start and end apart: 7, of which 6 were waited for; matrix products, arithmetic and copies ran while one was open for 7% of the time, Pallas kernels for 0%

profile of v1, /device:TPU:8, one launch (start us, length us, event | category | flops | bytes accessed | tf_op | source)
XLA Modules:
  0.0 342.0 jit_solution(9749674784945389611)
XLA Ops:
  7.2 0.7 all-gather.6.cloned.1.call-update
  7.9 0.7 all-gather.4.cloned.1.call-update
  8.7 0.7 all-gather.8.cloned.1.call-update
  9.4 0.7 select_reduce_fusion
  10.1 27.9 %all_gather.15 = f32[1024,8]{0,1:T(8,128)S(1)} all-gather(f32[128,8]{0,1:T(8,128)S(1)} %select_reduce_fusion), channel_id=1, replica_groups=mesh['dp'=4,'expert'=8] {'expert'}, dimensions={0}, use_global_device_ids=true | all-gather | bytes 36864 | tf_op jit(solution)/shard_map/all_gather | solution.py:26
  38.1 8.8 %all_gather.18 = bf16[1,384,1024]{2,1,0:T(8,128)(2,1)S(1)} all-gather(bf16[1,96,1024]{2,1,0:T(8,128)(2,1)} %param.10), channel_id=1, replica_groups=mesh['dp'=4,'expert'=8] {'dp'}, dimensions={1}, use_global_device_ids=true | all-gather | bytes 983040 | tf_op jit(solution)/shard_map/all_gather | solution.py:25
  46.9 34.9 %all-gather.4.cloned.1.call-done = bf16[1024,1024]{1,0:T(8,128)(2,1)} async-done(((bf16[128,1024]{1,0:T(8,128)(2,1)}), bf16[1024,1024]{1,0:T(8,128)(2,1)}) %all-gather.4.cloned.1.call-update) | async-done | bytes 2097168 | tf_op jit(solution)/shard_map/all_gather | solution.py:23
  81.8 5.5 %convolution_multiply_fusion = f32[1024,768]{0,1:T(8,128)} fusion(bf16[1024,1024]{1,0:T(8,128)(2,1)} %all-gather.4.cloned.1.call-done, bf16[1,1024,768]{2,1,0:T(8,128)(2,1)} %all-gather.6.cloned.1.call-done), kind=kOutput, calls=%fused_computation.5 | convolution fusion | flops 1611399168 | bytes 6815744 | tf_op jit(solution)/shard_map/dot_general | solution.py:32
  87.4 44.4 %all-gather.8.cloned.1.call-done = bf16[1024,1024]{1,0:T(8,128)(2,1)} async-done(((bf16[128,1024]{1,0:T(8,128)(2,1)}), bf16[1024,1024]{1,0:T(8,128)(2,1)}) %all-gather.8.cloned.1.call-update) | async-done | bytes 2097168 | tf_op jit(solution)/shard_map/all_gather | solution.py:24
  131.8 5.6 %multiply_convert_fusion.7 = (bf16[1024,384]{0,1:T(8,128)(2,1)}, bf16[1024,384]{0,1:T(8,128)(2,1)}, bf16[1024,384]{0,1:T(8,128)(2,1)S(1)}) fusion(f32[1024,768]{0,1:T(8,128)} %convolution_multiply_fusion, bf16[1,384,1024]{2,1,0:T(8,128)(2,1)S(1)} %all_gather.18, bf16[1024,1024]{1,0:T(8,128)(2,1)} %all-gather.8.cloned.1.call-done, f32[1024]{0:T(1024)S(1)} %bitcast.23), kind=kOutput, calls=%fused_computation.11 | convolution fusion | flops 815136768 | bytes 8392704 | tf_op jit(solution)/shard_map/dot_general | solution.py:39
  137.4 0.9 copy-done.4
  138.3 2.0 fusion.3
  140.4 4.4 %fusion.2 = bf16[1,1024,768]{1,2,0:T(8,128)(2,1)} fusion(bf16[1024,1024]{1,0:T(8,128)(2,1)S(1)} %copy-done.2, bf16[1024,384]{0,1:T(8,128)(2,1)} %get-tuple-element.17, bf16[1024,384]{0,1:T(8,128)(2,1)} %get-tuple-element.16), kind=kOutput, calls=%fused_computation.14 | convolution fusion | flops 1615331328 | bytes 5242880 | tf_op jit(solution)/shard_map/dot_general | solution.py:46
  144.8 5.2 %multiply_convert_fusion = bf16[1024,1024]{1,0:T(8,128)(2,1)} fusion(bf16[1,1024,768]{2,1,0:T(8,128)(2,1)} %all-gather.6.cloned.1.call-done, bf16[1024,384]{0,1:T(8,128)(2,1)} %get-tuple-element.17, bf16[1024,384]{0,1:T(8,128)(2,1)} %get-tuple-element.16), kind=kOutput, calls=%fused_computation | convolution fusion | flops 1615855616 | bytes 5242880 | tf_op jit(solution)/shard_map/dot_general | solution.py:43
  150.1 1.1 copy-done.5
  151.2 2.6 multiply_convert_fusion.2
  153.8 1.0 copy-done
  154.9 7.3 %reduce-scatter.11.cloned.1.call-done = bf16[1,96,1024]{2,1,0:T(8,128)(2,1)} async-done(((bf16[1,384,1024]{2,1,0:T(8,128)(2,1)}), bf16[1,96,1024]{2,1,0:T(8,128)(2,1)}) %reduce-scatter.11.cloned.1.call-update) | async-done | bytes 196624 | tf_op jit(solution)/shard_map/reduce_scatter | solution.py:54
  162.2 1.7 subtract_convert_fusion.1
  163.9 29.1 %reduce-scatter.9.cloned.1.call-done = bf16[1,256,768]{1,2,0:T(8,128)(2,1)} async-done(((bf16[1,1024,768]{1,2,0:T(8,128)(2,1)}), bf16[1,256,768]{1,2,0:T(8,128)(2,1)}) %reduce-scatter.9.cloned.1.call-update) | async-done | bytes 393232 | tf_op jit(solution)/shard_map/reduce_scatter | solution.py:53
  193.0 1.1 subtract_convert_fusion
  194.1 0.9 copy.19
  195.0 69.2 %reduce-scatter.7.cloned.1.call-done = bf16[128,1024]{1,0:T(8,128)(2,1)} async-done(((bf16[1024,1024]{1,0:T(8,128)(2,1)}), bf16[128,1024]{1,0:T(8,128)(2,1)}) %reduce-scatter.7.cloned.1.call-update) | async-done | bytes 262160 | tf_op jit(solution)/shard_map/reduce_scatter | solution.py:52
  264.2 70.9 %reduce-scatter.5.cloned.1.call-done = bf16[128,1024]{1,0:T(8,128)(2,1)} async-done(((bf16[1024,1024]{1,0:T(8,128)(2,1)}), bf16[128,1024]{1,0:T(8,128)(2,1)}) %reduce-scatter.5.cloned.1.call-update) | async-done | bytes 262160 | tf_op jit(solution)/shard_map/reduce_scatter | solution.py:51
  (23 shorter events, 0.5 us)
Async XLA Ops:
  7.2 39.8 %all-gather.6.cloned.1.call-start = ((), (), s32[]{:S(2)}) async-start(), calls=%async_computation.5 | async-start | bytes 1966080 | tf_op jit(solution)/shard_map/all_gather | solution.py:22
  7.9 74.0 %all-gather.4.cloned.1.call-start = ((), (), s32[]{:S(2)}) async-start(), calls=%async_computation.4 | async-start | bytes 2359296 | tf_op jit(solution)/shard_map/all_gather | solution.py:23
  8.6 123.1 %all-gather.8.cloned.1.call-start = ((), (), s32[]{:S(2)}) async-start(), calls=%async_computation.7 | async-start | bytes 2359296 | tf_op jit(solution)/shard_map/all_gather | solution.py:24
  9.4 152.9 %reduce-scatter.11.cloned.1.call-start = ((), (), s32[]{:S(2)}) async-start(), calls=%async_computation.10 | async-start | bytes 983040 | tf_op jit(solution)/shard_map/reduce_scatter | solution.py:54
  131.8 6.5 %copy-start.3 = (bf16[1024,1024]{1,0:T(8,128)(2,1)S(1)}, bf16[1024,1024]{1,0:T(8,128)(2,1)}, u32[]{:S(2)}) copy-start(bf16[1024,1024]{1,0:T(8,128)(2,1)} %all-gather.8.cloned.1.call-done) | copy-start | bytes 6291460
  137.4 0.9 copy-start.4
  138.3 2.1 copy-start.2
  140.3 52.6 %reduce-scatter.9.cloned.1.call-start = ((), (), s32[]{:S(2)}) async-start(), calls=%async_computation.9 | async-start | bytes 1966080 | tf_op jit(solution)/shard_map/reduce_scatter | solution.py:53
  144.8 119.4 %reduce-scatter.7.cloned.1.call-start = ((), (), s32[]{:S(2)}) async-start(), calls=%async_computation.8 | async-start | bytes 2359296 | tf_op jit(solution)/shard_map/reduce_scatter | solution.py:52
  150.0 1.1 copy-start.5
  150.1 185.1 %reduce-scatter.5.cloned.1.call-start = ((), (), s32[]{:S(2)}) async-start(), calls=%async_computation.6 | async-start | bytes 2359296 | tf_op jit(solution)/shard_map/reduce_scatter | solution.py:51
  153.8 1.0 copy-start
  153.8 8.5 %copy-start.1 = (bf16[1,96,1024]{2,1,0:T(8,128)(2,1)S(1)}, bf16[1,96,1024]{2,1,0:T(8,128)(2,1)}, u32[]{:S(2)}) copy-start(bf16[1,96,1024]{2,1,0:T(8,128)(2,1)} %param.10) | copy-start | bytes 589828
Sparse Core Ops, SparseCore 0:
  9.6 20.8 all-gather.5
  32.5 49.2 all-gather.3
  84.0 47.7 all-gather.7
  140.5 21.7 reduce-scatter.10
  164.8 28.1 reduce-scatter.8
  196.9 67.2 reduce-scatter.6
  268.3 66.7 reduce-scatter.4

commit v2 on v1

--- a/solution.py
+++ b/solution.py
@@ -1,6 +1,8 @@
 import jax
 import jax.numpy as jnp
 from jax import lax
+from jax.experimental import pallas as pl
+from jax.experimental.pallas import tpu as pltpu
 from jax.sharding import PartitionSpec as P
 
 step_rate = 0.5
@@ -57,9 +59,355 @@
     return (moe_out, token_grad, new_w_in, new_w_down)
 
 
+MESH = pl.DeviceIdType.MESH
+f32 = jnp.float32
+bf16 = jnp.bfloat16
+
+
+def xor4(z, j):
+    a, b, c, d = z // 2, z % 2, j // 2, j % 2
+    return 2 * (a + c - 2 * a * c) + b + d - 2 * b * d
+
+
+def fused_kernel(
+    tok_ref, grad_ref, g_ref, win_ref, wdown_ref,
+    moe_ref, back_ref, nwin_ref, nwdown_ref,
+    rows_all, g_all, win, wdown, dproj_all, act_all, dy_all, part, rx, rz,
+    gin, gdown, gin_core, gdown_core, gin_y, gdown_y,
+    g_send, g_recv, w_send, w_recv, z_send, x_send, row_recv,
+    rx_send, rx_recv, rz_send, rz_recv, gc_send, gc_recv, gy_send, gy_recv,
+):
+    dp = lax.axis_index("dp")
+    me = lax.axis_index("expert")
+    y, core = dp // 2, dp % 2
+    z, x = me // 2, me % 2
+    n = tok_ref.shape[0]
+    hidden = wdown.shape[0]
+    scale_in = win.shape[0] ** -0.5
+    scale_down = hidden**-0.5
+    q_in, q_down = win_ref.shape[0], wdown_ref.shape[0]
+    core_peer = (2 * y + 1 - core, me)
+    y_peer = (2 * (1 - y) + core, me)
+    x_peer = (dp, 2 * z + 1 - x)
+    inner = (z + 1) // 2 % 2
+
+    def copy(src, dst, ssem, rsem, device):
+        return pltpu.make_async_remote_copy(
+            src_ref=src, dst_ref=dst, send_sem=ssem, recv_sem=rsem,
+            device_id=device, device_id_type=MESH,
+        )
+
+    def rows(s, size):
+        return pl.ds(pl.multiple_of(s * size, 16), size)
+
+    def order(j):
+        far = j // 2
+        swapped = xor4(z, j + inner * far * (5 - 2 * j))
+        return swapped
+
+    rows_all[0, rows(me, n), :] = tok_ref[...]
+    rows_all[1, rows(me, n), :] = grad_ref[...]
+    g_all[me] = g_ref[...]
+    win[rows(dp, q_in), :] = win_ref[...]
+    wdown[rows(dp, q_down), :] = wdown_ref[...]
+
+    barrier = pltpu.get_barrier_semaphore()
+    for k in range(1, 8):
+        pl.semaphore_signal(barrier, inc=1, device_id=(dp, (me + k) % 8), device_id_type=MESH)
+    pl.semaphore_signal(barrier, inc=1, device_id=core_peer, device_id_type=MESH)
+    pl.semaphore_signal(barrier, inc=1, device_id=y_peer, device_id_type=MESH)
+    pl.semaphore_wait(barrier, 9)
+
+    def w_copy(w, k):
+        ref, size = ((win, q_in), (wdown, q_down))[w]
+        source = 2 * (1 - y) + core if k == 2 else dp
+        block = ref.at[rows(source, size), :]
+        return copy(block, block, w_send.at[w, k], w_recv.at[w, source], y_peer if k == 0 else core_peer)
+
+    def w_arrive(w, source):
+        ref, size = ((win, q_in), (wdown, q_down))[w]
+        block = ref.at[rows(source, size), :]
+        copy(block, block, w_send.at[w, 0], w_recv.at[w, source], y_peer).wait_recv()
+
+    def g_copy(k):
+        return copy(g_all.at[me], g_all.at[me], g_send.at[k - 1], g_recv.at[me], (dp, (me + k) % 8))
+
+    def z_copy(a, j, up):
+        s = order(j)
+        block = rows_all.at[a, rows(2 * s + x, n), :]
+        target = me + 2 if up else me - 2
+        return copy(block, block, z_send.at[a, j, up], row_recv.at[a, 2 * s + x], (dp, target))
+
+    def x_copy(a, j):
+        s = order(j)
+        block = rows_all.at[a, rows(2 * s + x, n), :]
+        return copy(block, block, x_send.at[a, j], row_recv.at[a, 2 * s + x], x_peer)
+
+    def row_arrive(a, slot):
+        block = rows_all.at[a, rows(slot, n), :]
+        copy(block, block, x_send.at[a, 0], row_recv.at[a, slot], x_peer).wait_recv()
+
+    def z_conditions(j):
+        s = order(j)
+        return (z < 3) & (s <= z), (z > 0) & (s >= z)
+
+    def forward(j):
+        go_up, go_down = z_conditions(j)
+        for a in range(2):
+            if j > 0:
+                row_arrive(a, 2 * order(j) + x)
+
+            @pl.when(go_up)
+            def _():
+                z_copy(a, j, 1).start()
+
+            @pl.when(go_down)
+            def _():
+                z_copy(a, j, 0).start()
+
+            x_copy(a, j).start()
+
+    for w in range(2):
+        w_copy(w, 0).start()
+        w_copy(w, 1).start()
+    for k in range(1, 8):
+        g_copy(k).start()
+    forward(0)
+    forward(1)
+    for w in range(2):
+        w_arrive(w, 2 * (1 - y) + core)
+        w_copy(w, 2).start()
+    forward(2)
+    for k in range(1, 8):
+        s = (me + k) % 8
+        copy(g_all.at[s], g_all.at[s], g_send.at[0], g_recv.at[s], x_peer).wait_recv()
+    for w in range(2):
+        w_arrive(w, 2 * y + 1 - core)
+        w_arrive(w, 2 * (1 - y) + 1 - core)
+
+    nt = (((1,), (1,)), ((), ()))
+    tn = (((0,), (0,)), ((), ()))
+
+    def compute(slot):
+        at = rows(slot, n)
+        by_expert = jnp.transpose(g_all[slot], (1, 0))
+        lane = lax.broadcasted_iota(jnp.int32, by_expert.shape, 1)
+        g = jnp.sum(jnp.where(lane == me, by_expert, 0.0), axis=1, keepdims=True)
+        dy = (g * rows_all[1, at, :].astype(f32)).astype(bf16)
+        dy_all[at, :] = dy
+        proj = jnp.dot(rows_all[0, at, :], win[...], preferred_element_type=f32) * scale_in
+        dact = lax.dot_general(dy, wdown[...], nt, preferred_element_type=f32) * scale_down
+        gate, up = proj[:, :hidden], proj[:, hidden:]
+        sig = jax.nn.sigmoid(gate)
+        silu = gate * sig
+        act = (silu * up).astype(bf16)
+        act_all[at, :] = act
+        dproj_all[at, :hidden] = (dact * up * sig * (1.0 + gate * (1.0 - sig))).astype(bf16)
+        dproj_all[at, hidden:] = (dact * silu).astype(bf16)
+        out = (jnp.dot(act, wdown[...], preferred_element_type=f32) * scale_down).astype(bf16)
+        part[0, at, :] = (g * out.astype(f32)).astype(bf16)
+        dx = lax.dot_general(dproj_all[at, :], win[...], nt, preferred_element_type=f32) * scale_in
+        part[1, at, :] = dx.astype(bf16)
+
+    def rx_copy(a, s):
+        block = part.at[a, rows(2 * s + 1 - x, n), :]
+        return copy(block, rx.at[a, s], rx_send.at[a, s], rx_recv.at[a, s], x_peer)
+
+    def step(j, carry):
+        @pl.when(j == 1)
+        def _():
+            forward(3)
+
+        s = order(j)
+        compute(2 * s + x)
+        row_arrive(0, 2 * s + 1 - x)
+        row_arrive(1, 2 * s + 1 - x)
+        compute(2 * s + 1 - x)
+        rx_copy(0, s).start()
+        rx_copy(1, s).start()
+        return carry
+
+    lax.fori_loop(0, 4, step, 0)
+
+    for q in range(4):
+        gin[q * q_in:(q + 1) * q_in, :] = (
+            lax.dot_general(rows_all[0, :, q * q_in:(q + 1) * q_in], dproj_all[...], tn, preferred_element_type=f32) * scale_in
+        ).astype(bf16)
+    gdown[...] = (lax.dot_general(act_all[...], dy_all[...], tn, preferred_element_type=f32) * scale_down).astype(bf16)
+
+    def gc_copy(w, yy):
+        ref, size, dst = ((gin, q_in, gin_core), (gdown, q_down, gdown_core))[w]
+        return copy(ref.at[rows(2 * yy + 1 - core, size), :], dst.at[yy], gc_send.at[w, yy], gc_recv.at[w, yy], core_peer)
+
+    def gy_copy(w):
+        ref, size, dst = ((gin, q_in, gin_y), (gdown, q_down, gdown_y))[w]
+        return copy(ref.at[rows(2 * (1 - y) + core, size), :], dst, gy_send.at[w], gy_recv.at[w], y_peer)
+
+    for w in range(2):
+        for yy in range(2):
+            gc_copy(w, yy).start()
+
+    def line_copy(a, t, up):
+        if up:
+            slot, target = t, me + 2
+        else:
+            slot, target = t + (4 - t) * (1 - jnp.minimum(z - 1 - t, 1)), me - 2
+        return copy(part.at[a, rows(2 * t + x, n), :], rz.at[a, slot], rz_send.at[a, t], rz_recv.at[a, slot], (dp, target))
+
+    def line_arrive(a, slot):
+        copy(rz.at[a, slot], rz.at[a, slot], rz_send.at[a, 0], rz_recv.at[a, slot], x_peer).wait_recv()
+
+    def line(t):
+        for a in range(2):
+            at = rows(2 * t + x, n)
+
+            @pl.when(z != t)
+            def _():
+                rx_copy(a, t).wait_recv()
+
+                @pl.when(((z < t) & (z > 0)) | ((z > t) & (z < 3)))
+                def _():
+                    line_arrive(a, t)
+                    part[a, at, :] = (
+                        part[a, at, :].astype(f32) + rx[a, t].astype(f32) + rz[a, t].astype(f32)
+                    ).astype(bf16)
+
+                @pl.when(((z < t) & (z == 0)) | ((z > t) & (z == 3)))
+                def _():
+                    part[a, at, :] = (part[a, at, :].astype(f32) + rx[a, t].astype(f32)).astype(bf16)
+
+            @pl.when(z < t)
+            def _():
+                line_copy(a, t, 1).start()
+
+            @pl.when(z > t)
+            def _():
+                line_copy(a, t, 0).start()
+
+    line(1)
+    line(2)
+    for w in range(2):
+        ref, size, got = ((gin, q_in, gin_core), (gdown, q_down, gdown_core))[w]
+        gc_copy(w, 0).wait_recv()
+        gc_copy(w, 1).wait_recv()
+        at = rows(2 * (1 - y) + core, size)
+        ref[at, :] = (ref[at, :].astype(f32) + got[1 - y].astype(f32)).astype(bf16)
+        gy_copy(w).start()
+    line(0)
+    line(3)
+
+    for w in range(2):
+        ref, size, got, far, old, new = (
+            (gin, q_in, gin_core, gin_y, win_ref, nwin_ref),
+            (gdown, q_down, gdown_core, gdown_y, wdown_ref, nwdown_ref),
+        )[w]
+        gy_copy(w).wait_recv()
+        total = ref[rows(dp, size), :].astype(f32) + got[y].astype(f32) + far[...].astype(f32)
+        new[...] = (old[...].astype(f32) - step_rate * total).astype(bf16)
+
+    for a in range(2):
+        out = (moe_ref, back_ref)[a]
+        rx_copy(a, z).wait_recv()
+        own = part[a, rows(me, n), :].astype(f32) + rx[a, z].astype(f32)
+
+        @pl.when(z == 0)
+        def _():
+            line_arrive(a, 4)
+            out[...] = (own + rz[a, 4].astype(f32)).astype(bf16)
+
+        @pl.when(z == 3)
+        def _():
+            line_arrive(a, 3)
+            out[...] = (own + rz[a, 3].astype(f32)).astype(bf16)
+
+        @pl.when((z > 0) & (z < 3))
+        def _():
+            line_arrive(a, z)
+            line_arrive(a, 4)
+            out[...] = (own + rz[a, z].astype(f32) + rz[a, 4].astype(f32)).astype(bf16)
+
+    for w in range(2):
+        for k in range(3):
+            w_copy(w, k).wait_send()
+        for yy in range(2):
+            gc_copy(w, yy).wait_send()
+        gy_copy(w).wait_send()
+    for k in range(1, 8):
+        g_copy(k).wait_send()
+    for a in range(2):
+        for j in range(4):
+            go_up, go_down = z_conditions(j)
+
+            @pl.when(go_up)
+            def _():
+                z_copy(a, j, 1).wait_send()
+
+            @pl.when(go_down)
+            def _():
+                z_copy(a, j, 0).wait_send()
+
+            x_copy(a, j).wait_send()
+            rx_copy(a, j).wait_send()
+
+            @pl.when(z < j)
+            def _():
+                line_copy(a, j, 1).wait_send()
+
+            @pl.when(z > j)
+            def _():
+                line_copy(a, j, 0).wait_send()
+
+
+def fused_body(tokens, routes, gates, w_in, w_down, out_grad):
+    n, width = tokens.shape
+    hidden = w_in.shape[2] // 2
+    q_in, q_down = w_in.shape[1], w_down.shape[1]
+    hit = routes.T[:, None, :] == jnp.arange(8, dtype=jnp.int32)[None, :, None]
+    weight = jnp.sum(jnp.where(hit, gates.T[:, None, :], 0.0), axis=0)
+    vmem = pl.BlockSpec(memory_space=pltpu.VMEM)
+    dma = pltpu.SemaphoreType.DMA
+    buf = pltpu.VMEM
+    outs = pl.pallas_call(
+        fused_kernel,
+        out_shape=(
+            jax.ShapeDtypeStruct((n, width), bf16),
+            jax.ShapeDtypeStruct((n, width), bf16),
+            jax.ShapeDtypeStruct((q_in, 2 * hidden), bf16),
+            jax.ShapeDtypeStruct((q_down, width), bf16),
+        ),
+        in_specs=[vmem] * 5,
+        out_specs=(vmem,) * 4,
+        scratch_shapes=[
+            buf((2, 8 * n, width), bf16),
+            buf((8, 8, n), f32),
+            buf((4 * q_in, 2 * hidden), bf16),
+            buf((4 * q_down, width), bf16),
+            buf((8 * n, 2 * hidden), bf16),
+            buf((8 * n, hidden), bf16),
+            buf((8 * n, width), bf16),
+            buf((2, 8 * n, width), bf16),
+            buf((2, 4, n, width), bf16),
+            buf((2, 5, n, width), bf16),
+            buf((4 * q_in, 2 * hidden), bf16),
+            buf((4 * q_down, width), bf16),
+            buf((2, q_in, 2 * hidden), bf16),
+            buf((2, q_down, width), bf16),
+            buf((q_in, 2 * hidden), bf16),
+            buf((q_down, width), bf16),
+            dma((7,)), dma((8,)), dma((2, 3)), dma((2, 4)), dma((2, 4, 2)), dma((2, 4)), dma((2, 8)),
+            dma((2, 4)), dma((2, 4)), dma((2, 4)), dma((2, 5)), dma((2, 2)), dma((2, 2)), dma((2,)), dma((2,)),
+        ],
+        compiler_params=pltpu.CompilerParams(
+            collective_id=0, has_side_effects=True, vmem_limit_bytes=48 * 1024 * 1024
+        ),
+    )(tokens, out_grad, weight, w_in[0], w_down[0])
+    return (outs[0], outs[1], outs[2][None], outs[3][None])
+
+
 def solution(mesh):
+    fused = mesh.shape["dp"] == 4 and mesh.shape["expert"] == 8
     return jax.shard_map(
-        body,
+        fused_body if fused else body,
         mesh=mesh,
         in_specs=(
             P(("dp", "expert"), None),

time: 345 us -> 148 us (0.43)
  the two profiles are of different devices: /device:TPU:8 before, /device:TPU:28 now
where the time goes in v2:
time: 148 us
  Pallas kernels  140 us (95%)
  local copies, waits for them, and re-layouts  7.33 us (5%)
    pallas_call x1, Pallas kernels, fused_body(): pl.pallas_call(fused_kernel, out_shape=(jax.ShapeDtypeStruct((n, width),...  140 us
    unnamed x16, local copies, waits for them, and re-layouts  7.33 us

profile of v2, /device:TPU:28, one launch (start us, length us, event | category | flops | bytes accessed | tf_op | source)
XLA Modules:
  0.0 147.6 jit_solution(8834410816661276509)
XLA Ops:
  0.6 0.0 copy-start.5
  0.6 0.0 copy-start.4
  0.7 0.7 copy-done.5
  1.3 0.0 copy-done.4
  1.3 0.0 copy-start
  1.3 1.0 copy-done
  2.3 0.0 copy-start.1
  2.3 0.9 copy-done.1
  3.3 0.0 copy-start.2
  3.3 0.9 copy-done.2
  4.2 0.0 copy-start.3
  4.2 0.9 copy-done.3
  5.2 139.6 %shard_map.93 = (bf16[128,1024]{1,0:T(8,128)(2,1)S(1)}, bf16[128,1024]{1,0:T(8,128)(2,1)S(1)}, bf16[256,768]{1,0:T(8,128)(2,1)S(1)}, bf16[96,1024]{1,0:T(8,128)(2,1)S(1)}) custom-call(bf16[128,1024]{1,0:T(8,128)(2,1)S(1)} %copy-done.1, bf16[128,1024]{1,0:T(8,128)(2,1)S(1)} %copy-done.2, f32[8,128]{1,0:T(8,128)S(1)} %select_reduce_fusion.g_ref, ...), custom_call_target="tpu_custom_call" | custom-call | tf_op jit(solution)/shard_map/pallas_call | solution.py:370
  144.8 0.7 copy.14
  145.5 0.7 copy.15
  146.2 0.7 copy.16
  146.9 0.7 copy.17
  (1 shorter events, 0.0 us)
Async XLA Ops:
  0.6 0.7 copy-start.5
  0.6 0.7 copy-start.4
  1.3 1.0 copy-start
  2.3 0.9 copy-start.1
  3.3 0.9 copy-start.2
  4.2 0.9 copy-start.3

commit v3 on v2

--- a/solution.py
+++ b/solution.py
@@ -223,11 +223,12 @@
         row_arrive(0, 2 * s + 1 - x)
         row_arrive(1, 2 * s + 1 - x)
         compute(2 * s + 1 - x)
-        rx_copy(0, s).start()
-        rx_copy(1, s).start()
         return carry
 
     lax.fori_loop(0, 4, step, 0)
+    for j in (3, 2, 1, 0):
+        for a in range(2):
+            rx_copy(a, order(j)).start()
 
     for q in range(4):
         gin[q * q_in:(q + 1) * q_in, :] = (
@@ -284,8 +285,8 @@
             def _():
                 line_copy(a, t, 0).start()
 
-    line(1)
-    line(2)
+    line(3)
+    line(0)
     for w in range(2):
         ref, size, got = ((gin, q_in, gin_core), (gdown, q_down, gdown_core))[w]
         gc_copy(w, 0).wait_recv()
@@ -293,8 +294,8 @@
         at = rows(2 * (1 - y) + core, size)
         ref[at, :] = (ref[at, :].astype(f32) + got[1 - y].astype(f32)).astype(bf16)
         gy_copy(w).start()
-    line(0)
-    line(3)
+    line(2)
+    line(1)
 
     for w in range(2):
         ref, size, got, far, old, new = (

time: 148 us -> 121 us (0.82)
  the two profiles are of different devices: /device:TPU:28 before, /device:TPU:8 now
where the time goes in v3:
time: 121 us
  Pallas kernels  113 us (93%)
  local copies, waits for them, and re-layouts  7.33 us (6%)
    pallas_call x1, Pallas kernels, fused_body(): pl.pallas_call(fused_kernel, out_shape=(jax.ShapeDtypeStruct((n, width),...  113 us
    unnamed x16, local copies, waits for them, and re-layouts  7.33 us

profile of v3, /device:TPU:8, one launch (start us, length us, event | category | flops | bytes accessed | tf_op | source)
XLA Modules:
  0.0 120.6 jit_solution(3774748029387182464)
XLA Ops:
  0.6 0.0 copy-start.5
  0.6 0.0 copy-start.4
  0.7 0.7 copy-done.5
  1.3 0.0 copy-done.4
  1.3 0.0 copy-start
  1.3 1.0 copy-done
  2.3 0.0 copy-start.1
  2.3 0.9 copy-done.1
  3.3 0.0 copy-start.2
  3.3 0.9 copy-done.2
  4.2 0.0 copy-start.3
  4.2 0.9 copy-done.3
  5.2 112.6 %shard_map.93 = (bf16[128,1024]{1,0:T(8,128)(2,1)S(1)}, bf16[128,1024]{1,0:T(8,128)(2,1)S(1)}, bf16[256,768]{1,0:T(8,128)(2,1)S(1)}, bf16[96,1024]{1,0:T(8,128)(2,1)S(1)}) custom-call(bf16[128,1024]{1,0:T(8,128)(2,1)S(1)} %copy-done.1, bf16[128,1024]{1,0:T(8,128)(2,1)S(1)} %copy-done.2, f32[8,128]{1,0:T(8,128)S(1)} %select_reduce_fusion.g_ref, ...), custom_call_target="tpu_custom_call" | custom-call | tf_op jit(solution)/shard_map/pallas_call | solution.py:371
  117.8 0.7 copy.14
  118.5 0.7 copy.15
  119.2 0.7 copy.16
  120.0 0.7 copy.17
  (1 shorter events, 0.0 us)
Async XLA Ops:
  0.6 0.7 copy-start.5
  0.6 0.7 copy-start.4
  1.3 1.0 copy-start
  2.3 0.9 copy-start.1
  3.3 0.9 copy-start.2
  4.2 0.9 copy-start.3

commit v4 on v3

--- a/solution.py
+++ b/solution.py
@@ -226,8 +226,8 @@
         return carry
 
     lax.fori_loop(0, 4, step, 0)
-    for j in (3, 2, 1, 0):
-        for a in range(2):
+    for a in range(2):
+        for j in (3, 2, 1, 0):
             rx_copy(a, order(j)).start()
 
     for q in range(4):
@@ -258,8 +258,8 @@
     def line_arrive(a, slot):
         copy(rz.at[a, slot], rz.at[a, slot], rz_send.at[a, 0], rz_recv.at[a, slot], x_peer).wait_recv()
 
-    def line(t):
-        for a in range(2):
+    def line(a, t):
+        if True:
             at = rows(2 * t + x, n)
 
             @pl.when(z != t)
@@ -285,8 +285,6 @@
             def _():
                 line_copy(a, t, 0).start()
 
-    line(3)
-    line(0)
     for w in range(2):
         ref, size, got = ((gin, q_in, gin_core), (gdown, q_down, gdown_core))[w]
         gc_copy(w, 0).wait_recv()
@@ -294,8 +292,9 @@
         at = rows(2 * (1 - y) + core, size)
         ref[at, :] = (ref[at, :].astype(f32) + got[1 - y].astype(f32)).astype(bf16)
         gy_copy(w).start()
-    line(2)
-    line(1)
+    for a in range(2):
+        for t in (3, 0, 2, 1):
+            line(a, t)
 
     for w in range(2):
         ref, size, got, far, old, new = (

time: 121 us -> 119 us (0.983); the launches traced: 121 us -> 116 us
  Pallas kernels: 113 us -> 108 us
    pallas_call x1, Pallas kernels: 113 us -> 108 us  [fused_body(): pl.pallas_call(fused_kernel, out_shape=(jax.ShapeDtypeStruct((n, width),...]
where the time goes in v4:
time: 119 us; the launch traced here: 116 us
  Pallas kernels  108 us (91%)
  local copies, waits for them, and re-layouts  7.33 us (6%)
    pallas_call x1, Pallas kernels, fused_body(): pl.pallas_call(fused_kernel, out_shape=(jax.ShapeDtypeStruct((n, width),...  108 us
    unnamed x16, local copies, waits for them, and re-layouts  7.33 us

profile of v4, /device:TPU:8, one launch (start us, length us, event | category | flops | bytes accessed | tf_op | source)
XLA Modules:
  0.0 116.3 jit_solution(8979476479692660354)
XLA Ops:
  0.6 0.0 copy-start.5
  0.6 0.0 copy-start.4
  0.7 0.7 copy-done.5
  1.3 0.0 copy-done.4
  1.3 0.0 copy-start
  1.3 1.0 copy-done
  2.3 0.0 copy-start.1
  2.3 0.9 copy-done.1
  3.3 0.0 copy-start.2
  3.3 0.9 copy-done.2
  4.2 0.0 copy-start.3
  4.2 0.9 copy-done.3
  5.2 108.3 %shard_map.93 = (bf16[128,1024]{1,0:T(8,128)(2,1)S(1)}, bf16[128,1024]{1,0:T(8,128)(2,1)S(1)}, bf16[256,768]{1,0:T(8,128)(2,1)S(1)}, bf16[96,1024]{1,0:T(8,128)(2,1)S(1)}) custom-call(bf16[128,1024]{1,0:T(8,128)(2,1)S(1)} %copy-done.1, bf16[128,1024]{1,0:T(8,128)(2,1)S(1)} %copy-done.2, f32[8,128]{1,0:T(8,128)S(1)} %select_reduce_fusion.g_ref, ...), custom_call_target="tpu_custom_call" | custom-call | tf_op jit(solution)/shard_map/pallas_call | solution.py:370
  113.5 0.7 copy.14
  114.2 0.7 copy.15
  114.9 0.7 copy.16
  115.7 0.7 copy.17
  (1 shorter events, 0.0 us)
Async XLA Ops:
  0.6 0.7 copy-start.5
  0.6 0.7 copy-start.4
  1.3 1.0 copy-start
  2.3 0.9 copy-start.1
  3.3 0.9 copy-start.2
  4.2 0.9 copy-start.3
